TPU v7x, 128 devices: a whole 4x4x4 slice. The times are simulated.
128 devices in a mesh: tm: 8 (over y, core), space: 16 (over z, x).
Axes of the slice: x: 4, y: 4, z: 4, core: 2. Of those that a mesh axis runs over, the one named last changes fastest.
Arguments:
- vorticity: float32 [512, 8192], P('space'), may hold values from -6 to 6
- stream: float32 [512, 8192], P('space'), may hold values from -0.8 to 0.8
- forcing: float32 [512, 8192], P('space'), may hold values from -1.2 to 1.2, as said below
- conv_in: float32 [8, 3, 3], replicated, may hold values from -2 to 2
- conv_out: float32 [8, 3, 3], replicated, may hold values from -0.75 to 0.75
Outputs:
- slice_ends: float32 [8, 512, 8192], P('tm', 'space')
Inputs may be any that keep to these rules, and one draw needn't show every extreme that they name: `forcing`: a vorticity source field.
All inputs are finite; a program needn't handle non-finite values.
Results may differ from a plain program's by a relative error of at most 0.0001.
Values sent between devices are 32-bit elements; how exact they have to be, the bound alone decides.
A program may use at most 128 MiB of HBM per device.

v0:
```python
import jax
import jax.numpy as jnp
from jax import lax
from jax.sharding import PartitionSpec as P

STEPS = 4
ITERS = 2


time_step = 1.0
viscosity = 0.1
drag_rate = 0.05
coarse_gain = 0.5


def with_halo(value, sides, width):
    for axis, dim in sides:
        size, length = (lax.axis_size(axis), value.shape[dim])
        up = [(i, (i + 1) % size) for i in range(size)]
        down = [(j, i) for i, j in up]
        last = lax.slice_in_dim(value, length - width, length, axis=dim)
        first = lax.slice_in_dim(value, 0, width, axis=dim)
        before = lax.ppermute(last, axis, up)
        after = lax.ppermute(first, axis, down)
        value = jnp.concatenate([before, value, after], axis=dim)
    return value


def shifted(block, axis, distance):
    devices = range(lax.axis_size(axis))
    route = [(i - distance, i) for i in devices if i - distance in devices]
    return lax.ppermute(block, axis, route)


def field_rhs(padded, vel_x, vel_y, source):
    centre = padded[..., 1:-1, :]
    right = jnp.roll(centre, -1, axis=-1)
    left = jnp.roll(centre, 1, axis=-1)
    above = padded[..., 2:, :]
    below = padded[..., :-2, :]
    grad_x = (right - left) * 0.5
    grad_y = (above - below) * 0.5
    laplace = above + below + right + left - 4.0 * centre
    return -(vel_x * grad_x + vel_y * grad_y) + viscosity * laplace - drag_rate * centre + source


def restrict(values):
    row_count, col_count = (values.shape[-2], values.shape[-1])
    blocks = values.reshape((row_count // 4, 4, col_count // 4, 4))
    return jnp.mean(blocks, axis=(-3, -1))


def prolong(coarse):
    return jnp.repeat(jnp.repeat(coarse, 4, axis=-2), 4, axis=-1)


def spread(padded, conv_in):
    row_count = padded.shape[0] - 2
    summed = jnp.zeros((conv_in.shape[0], row_count, padded.shape[1]), jnp.float32)
    for row_shift in range(3):
        for col_shift in range(3):
            moved = jnp.roll(padded[row_shift : row_shift + row_count], 1 - col_shift, axis=-1)
            summed = summed + conv_in[:, row_shift, col_shift][:, None, None] * moved[None]
    return summed


def collect(hidden, conv_out):
    row_count = hidden.shape[1] - 2
    summed = jnp.zeros((row_count, hidden.shape[2]), jnp.float32)
    for row_shift in range(3):
        for col_shift in range(3):
            moved = jnp.roll(hidden[:, row_shift : row_shift + row_count], 1 - col_shift, axis=-1)
            summed = summed + jnp.sum(
                conv_out[:, row_shift, col_shift][:, None, None] * moved, axis=0
            )
    return summed


def coarse_advance(padded, conv_in, conv_out):
    hidden = jnp.tanh(spread(padded, conv_in))
    return padded[2:-2] + coarse_gain * collect(hidden, conv_out)


def body(vorticity, stream, forcing, conv_in, conv_out):
    time_slot = lax.axis_index("tm")
    chain_length = lax.axis_size("tm")
    edge_rows = with_halo(jnp.stack([stream, forcing]), (("space", 1),), 4)
    stream_ext = edge_rows[0]
    centre = stream_ext[1:-1]
    vel_x = (stream_ext[2:] - stream_ext[:-2]) * 0.5
    vel_y = -(jnp.roll(centre, -1, axis=-1) - jnp.roll(centre, 1, axis=-1)) * 0.5
    source = edge_rows[1][1:-1]

    def coarse_step(coarse):
        padded = with_halo(coarse, (("space", 0),), 2)
        return coarse_advance(padded, conv_in, conv_out)

    first_coarse = restrict(vorticity)

    def run_chain(corrections):

        def relay_turn(position, coarse):
            advanced = coarse_step(coarse)
            received = shifted(advanced + corrections, "tm", 1)
            return jnp.where(time_slot == 0, first_coarse, received)

        coarse = lax.fori_loop(0, chain_length - 1, relay_turn, first_coarse)
        return (coarse, coarse_step(coarse))

    def section_rhs(state):
        padded = with_halo(state, (("space", 0),), 1)
        return field_rhs(padded, vel_x[3:-3], vel_y[3:-3], source[3:-3])

    own_coarse, g_old = run_chain(jnp.zeros_like(first_coarse))
    starts = jnp.where(time_slot == 0, vorticity, prolong(own_coarse))
    slice_ends = starts
    for iteration in range(ITERS):
        fine_state = starts
        for counter in range(STEPS):
            slope_one = section_rhs(fine_state)
            slope_two = section_rhs(fine_state + 0.5 * time_step * slope_one)
            slope_three = section_rhs(fine_state + 0.5 * time_step * slope_two)
            slope_four = section_rhs(fine_state + time_step * slope_three)
            fine_state = fine_state + time_step / 6.0 * (
                slope_one + 2.0 * slope_two + 2.0 * slope_three + slope_four
            )
        corrections = restrict(fine_state) - g_old
        own_coarse, g_new = run_chain(corrections)
        slice_ends = fine_state + prolong(g_new - g_old)
        if iteration + 1 < ITERS:
            moved = shifted(slice_ends, "tm", 1)
            starts = jnp.where(time_slot == 0, vorticity, moved)
        g_old = g_new
    return slice_ends[None]


def solution(mesh):
    placed = (P("space", None), P("space", None), P("space", None), P(), P())
    return jax.shard_map(
        body, mesh=mesh, in_specs=placed, out_specs=P("tm", "space", None), check_vma=False
    )
```

profile of v0, /device:TPU:1, one launch (start us, length us, event | category | flops | bytes accessed | tf_op | source)
XLA Modules:
  0.0 974.0 jit_solution(2356445318523904873)
XLA Ops:
  0.0 52.1 %reshape.91 = f32[8,4,2048,4]{3,2,1,0:T(8,128)} reshape(f32[32,8192]{1,0:T(8,128)} %param.11) | data formatting | bytes 2097152 | tf_op jit(solution)/shard_map/reshape | solution.py:49
  52.1 12.2 %reduce_sum.567 = f32[8,2048]{1,0:T(8,128)S(1)} reduce(f32[8,4,2048,4]{3,2,1,0:T(8,128)} %reshape.91, f32[]{:T(128)} %constant.81.clone.1), dimensions={1,3}, to_apply=%region_0.1 | reduce | flops 245760 | bytes 1114116 | tf_op jit(solution)/shard_map/reduce_sum | solution.py:50
  64.3 121.4 %while.36 = (s32[]{:T(128)}, f32[8,2048]{1,0:T(8,128)S(1)}, pred[]{:T(512)}, f32[8,3,3]{0,2,1:T(4,128)S(1)}, f32[8,3,3]{0,2,1:T(4,128)S(1)}, /*index=5*/f32[8,2048]{1,0:T(8,128)S(1)}, s32[]{:T(128)}) while((s32[]{:T(128)}, f32[8,2048]{1,0:T(8,128)S(1)}, pred[]{:T(512)}, f32[8,3,3]{0,2,1:T(4,128)S(1)}, f32[8,3,3]{0,2,1:T(4,128)S(1)}, ...), condition=%wide.region_11.12_spmd, body=%wide.region_1.11_spmd.sunk | while | flops 6279170 | bytes 17041044 | solution.py:107
  64.4 6.8 collective-permute-start
  96.7 5.5 collective-permute-start.2
  113.1 5.5 collective-permute-start.2
  129.6 5.5 collective-permute-start.2
  146.0 5.5 collective-permute-start.2
  162.4 5.5 collective-permute-start.2
  178.9 5.5 collective-permute-start.2
  366.2 52.1 %reshape.94 = f32[8,4,2048,4]{3,2,1,0:T(8,128)} reshape(f32[32,8192]{1,0:T(8,128)} %multiply_add_fusion.17) | data formatting | bytes 2097152 | tf_op jit(solution)/shard_map/reshape | solution.py:49
  418.3 12.2 %reduce_sum.568 = f32[8,2048]{1,0:T(8,128)S(1)} reduce(f32[8,4,2048,4]{3,2,1,0:T(8,128)} %reshape.94, f32[]{:T(128)} %constant.81.clone.1), dimensions={1,3}, to_apply=%region_12.13 | reduce | flops 245760 | bytes 1114116 | tf_op jit(solution)/shard_map/reduce_sum | solution.py:50
  432.2 135.7 %while.37 = (s32[]{:T(128)}, f32[8,2048]{1,0:T(8,128)S(1)}, pred[]{:T(512)}, f32[8,3,3]{0,2,1:T(4,128)S(1)}, f32[8,3,3]{0,2,1:T(4,128)S(1)}, /*index=5*/f32[8,2048]{1,0:T(8,128)S(1)}, f32[8,2048]{1,0:T(8,128)S(1)}, s32[]{:T(128)}) while((s32[]{:T(128)}, f32[8,2048]{1,0:T(8,128)S(1)}, pred[]{:T(512)}, f32[8,3,3]{0,2,1:T(4,128)S(1)}, ...), condition=%wide.region_32.33_spmd, body=%wide.region_22.32_spmd.sunk | while | flops 6295554 | bytes 17106588 | solution.py:107
  441.7 26.4 %collective-permute-start.5 = (f32[8,2048]{1,0:T(8,128)S(1)}, f32[8,2048]{1,0:T(8,128)S(1)}, u32[]{:S(2)}, u32[]{:S(2)}) collective-permute-start(f32[8,2048]{1,0:T(8,128)S(1)} %add_add_fusion.4), channel_id=1, source_target_pairs={{0,16},{16,32},{32,48},{48,64},{64,80},{80,96},{96,112},{1,17},{17... | collective-permute-start | bytes 196616 | tf_op jit(solution)/shard_map/while/body/eval_jaxpr/ppermute | solution.py:32
  479.0 5.5 collective-permute-start.5
  495.4 5.5 collective-permute-start.5
  511.8 5.5 collective-permute-start.5
  528.2 5.5 collective-permute-start.5
  544.6 5.5 collective-permute-start.5
  561.1 5.5 collective-permute-start.5
  590.6 5.5 collective-permute-start.47
  596.1 11.7 %collective-permute-done.47 = f32[32,8192]{1,0:T(8,128)S(1)} collective-permute-done((f32[32,8192]{1,0:T(8,128)S(1)}, f32[32,8192]{1,0:T(8,128)S(1)}, u32[]{:S(2)}, u32[]{:S(2)}) %collective-permute-start.47) | collective-permute-done | bytes 1048608 | tf_op jit(solution)/shard_map/ppermute | solution.py:32
  756.4 52.1 %reshape.97 = f32[8,4,2048,4]{3,2,1,0:T(8,128)} reshape(f32[32,8192]{1,0:T(8,128)} %multiply_add_fusion.1) | data formatting | bytes 2097152 | tf_op jit(solution)/shard_map/reshape | solution.py:49
  808.4 12.2 %reduce_sum.587 = f32[8,2048]{1,0:T(8,128)S(1)} reduce(f32[8,4,2048,4]{3,2,1,0:T(8,128)} %reshape.97, f32[]{:T(128)} %constant.81.clone.1), dimensions={1,3}, to_apply=%region_42.43 | reduce | flops 245760 | bytes 1114116 | tf_op jit(solution)/shard_map/reduce_sum | solution.py:50
  820.6 135.6 %while.38 = (s32[]{:T(128)}, f32[8,2048]{1,0:T(8,128)S(1)}, pred[]{:T(512)}, f32[8,3,3]{0,2,1:T(4,128)S(1)}, f32[8,3,3]{0,2,1:T(4,128)S(1)}, /*index=5*/f32[8,2048]{1,0:T(8,128)S(1)}, f32[8,2048]{1,0:T(8,128)S(1)}, s32[]{:T(128)}) while((s32[]{:T(128)}, f32[8,2048]{1,0:T(8,128)S(1)}, pred[]{:T(512)}, f32[8,3,3]{0,2,1:T(4,128)S(1)}, ...), condition=%wide.region_53.54_spmd, body=%wide.region_43.53_spmd.sunk | while | flops 6295554 | bytes 17106588 | solution.py:107
  830.2 26.1 %collective-permute-start.8 = (f32[8,2048]{1,0:T(8,128)S(1)}, f32[8,2048]{1,0:T(8,128)S(1)}, u32[]{:S(2)}, u32[]{:S(2)}) collective-permute-start(f32[8,2048]{1,0:T(8,128)S(1)} %add_add_fusion.5), channel_id=1, source_target_pairs={{0,16},{16,32},{32,48},{48,64},{64,80},{80,96},{96,112},{1,17},{17... | collective-permute-start | bytes 196616 | tf_op jit(solution)/shard_map/while/body/eval_jaxpr/ppermute | solution.py:32
  867.3 5.5 collective-permute-start.8
  883.6 5.5 collective-permute-start.8
  900.0 5.5 collective-permute-start.8
  916.5 5.5 collective-permute-start.8
  932.9 5.5 collective-permute-start.8
  949.3 5.5 collective-permute-start.8
  (1168 shorter events, 599.6 us)
Async XLA Ops:
  64.4 7.7 collective-permute-start
  80.6 6.5 collective-permute-start.2
  96.7 6.8 collective-permute-start.2
  113.1 6.8 collective-permute-start.2
  129.6 6.8 collective-permute-start.2
  146.0 6.8 collective-permute-start.2
  162.4 6.8 collective-permute-start.2
  178.9 6.8 collective-permute-start.2
  194.6 25.5 %collective-permute-start.12 = (f32[1,8192]{1,0:T(1,128)}, f32[1,8192]{1,0:T(1,128)}, u32[]{:S(2)}, u32[]{:S(2)}) collective-permute-start(f32[1,8192]{1,0:T(1,128)} %get-tuple-element.753), channel_id=1, source_target_pairs={{0,1},{1,2},{2,3},{3,4},{4,5},{5,6},{6,7},{7,8},{8,9},{9,10},{10,1... | collective-permute-start | bytes 98312 | tf_op jit(solution)/shard_map/ppermute | solution.py:23
  194.6 25.5 %collective-permute-start.11 = (f32[1,8192]{1,0:T(1,128)}, f32[1,8192]{1,0:T(1,128)}, u32[]{:S(2)}, u32[]{:S(2)}) collective-permute-start(f32[1,8192]{1,0:T(1,128)} %get-tuple-element.752), channel_id=1, source_target_pairs={{1,0},{2,1},{3,2},{4,3},{5,4},{6,5},{7,6},{8,7},{9,8},{10,9},{11,1... | collective-permute-start | bytes 98312 | tf_op jit(solution)/shard_map/ppermute | solution.py:24
  200.3 17.7 %collective-permute-start.10 = (f32[2,4,8192]{2,1,0:T(4,128)}, f32[2,4,8192]{2,1,0:T(4,128)}, u32[]{:S(2)}, u32[]{:S(2)}) collective-permute-start(f32[2,4,8192]{2,1,0:T(4,128)} %get-tuple-element.521), channel_id=1, source_target_pairs={{1,0},{2,1},{3,2},{4,3},{5,4},{6,5},{7,6},{8,7},{9,8},{10,9},{11,1... | collective-permute-start | bytes 786440 | tf_op jit(solution)/shard_map/ppermute | solution.py:24
  203.7 6.4 collective-permute-start.43
  206.1 11.9 %collective-permute-start.9 = (f32[2,4,8192]{2,1,0:T(4,128)}, f32[2,4,8192]{2,1,0:T(4,128)S(1)}, u32[]{:S(2)}, u32[]{:S(2)}) collective-permute-start(f32[2,4,8192]{2,1,0:T(4,128)} %get-tuple-element.520), channel_id=1, source_target_pairs={{0,1},{1,2},{2,3},{3,4},{4,5},{5,6},{6,7},{7,8},{8,9},{9,10},{10,1... | collective-permute-start | bytes 786440 | tf_op jit(solution)/shard_map/ppermute | solution.py:23
  244.8 6.5 collective-permute-start.18
  356.3 6.5 collective-permute-start.42
  441.7 27.7 %collective-permute-start.5 = (f32[8,2048]{1,0:T(8,128)S(1)}, f32[8,2048]{1,0:T(8,128)S(1)}, u32[]{:S(2)}, u32[]{:S(2)}) collective-permute-start(f32[8,2048]{1,0:T(8,128)S(1)} %add_add_fusion.4), channel_id=1, source_target_pairs={{0,16},{16,32},{32,48},{48,64},{64,80},{80,96},{96,112},{1,17},{17... | collective-permute-start | bytes 196616 | tf_op jit(solution)/shard_map/while/body/eval_jaxpr/ppermute | solution.py:32
  479.0 6.8 collective-permute-start.5
  495.4 6.8 collective-permute-start.5
  511.8 6.8 collective-permute-start.5
  528.2 6.8 collective-permute-start.5
  544.6 6.8 collective-permute-start.5
  561.1 6.8 collective-permute-start.5
  590.6 17.2 %collective-permute-start.47 = (f32[32,8192]{1,0:T(8,128)S(1)}, f32[32,8192]{1,0:T(8,128)S(1)}, u32[]{:S(2)}, u32[]{:S(2)}) collective-permute-start(f32[32,8192]{1,0:T(8,128)S(1)} %add.1341), channel_id=1, source_target_pairs={{0,16},{16,32},{32,48},{48,64},{64,80},{80,96},{96,112},{1,17},{17... | collective-permute-start | bytes 3145736 | tf_op jit(solution)/shard_map/ppermute | solution.py:32
  689.6 6.4 collective-permute-start.67
  734.1 6.4 collective-permute-start.77
  830.2 27.5 %collective-permute-start.8 = (f32[8,2048]{1,0:T(8,128)S(1)}, f32[8,2048]{1,0:T(8,128)S(1)}, u32[]{:S(2)}, u32[]{:S(2)}) collective-permute-start(f32[8,2048]{1,0:T(8,128)S(1)} %add_add_fusion.5), channel_id=1, source_target_pairs={{0,16},{16,32},{32,48},{48,64},{64,80},{80,96},{96,112},{1,17},{17... | collective-permute-start | bytes 196616 | tf_op jit(solution)/shard_map/while/body/eval_jaxpr/ppermute | solution.py:32
  867.3 6.8 collective-permute-start.8
  883.6 6.8 collective-permute-start.8
  900.0 6.8 collective-permute-start.8
  916.5 6.8 collective-permute-start.8
  932.9 6.8 collective-permute-start.8
  949.3 6.8 collective-permute-start.8
  (173 other events, 793.9 us)
where the time goes:
time: 985 us; the launch traced here: 974 us
  starting transfers between devices  366 us (37%)
  local copies, waits for them, and re-layouts  223 us (23%)
  waiting for transfers between devices  219 us (22%)
  other arithmetic  161 us (16%)
    ppermute x57, starting transfers between devices, with_halo(): after = lax.ppermute(first, axis, down)  166 us
    ppermute x22, starting transfers between devices, shifted(): return lax.ppermute(block, axis, route)  163 us
    reshape x3, local copies, waits for them, and re-layouts, restrict(): blocks = values.reshape((row_count // 4, 4, col_count // 4, 4))  156 us
    ppermute x57, waiting for transfers between devices, with_halo(): before = lax.ppermute(last, axis, up)  142 us
    ppermute x22, waiting for transfers between devices, shifted(): return lax.ppermute(block, axis, route)  39.2 us
    ppermute x57, waiting for transfers between devices, with_halo(): after = lax.ppermute(first, axis, down)  37.4 us
    ppermute x57, starting transfers between devices, with_halo(): before = lax.ppermute(last, axis, up)  37.2 us
    reduce_sum x3, other arithmetic, restrict(): return jnp.mean(blocks, axis=(-3, -1))  36.6 us
  transfers between devices with their start and end apart: 136, of which 110 were waited for; matrix products, arithmetic and copies ran while one was open for 2% of the time, Pallas kernels for 0%

commit v1 on v0

v1 whole, which is shorter than its diff:
```python
import functools
import math

import jax
import jax.numpy as jnp
import numpy as np
from jax import lax
from jax.experimental import pallas as pl
from jax.experimental.pallas import tpu as pltpu
from jax.sharding import PartitionSpec as P

F32 = jnp.float32
VMEM = pltpu.VMEM
MESH = pl.DeviceIdType.MESH
HIGH = lax.Precision.HIGHEST

STEPS = 4
SLICES = 8
LANES = 128
CHUNK = 64
INNER = 32
HALO = 16
PAD = 8
TALL = INNER + 2 * HALO + 2 * PAD
OWN = PAD + HALO
PITCH = 33
BLOCKS = 16
REACH = 28
WINDOW = 2 * REACH


def fine_weights():
    shift = np.polynomial.Polynomial([-0.45, 0.2])
    of_w = sum(shift**j / math.factorial(j) for j in range(5))
    of_f = sum(shift**j / math.factorial(j + 1) for j in range(4))
    return [float(v) for v in of_w.coef], [float(v) for v in of_f.coef] + [0.0]


def lane_iota():
    return lax.broadcasted_iota(jnp.int32, (8, LANES), 1)


def lane_shifted(value, up):
    lane = lax.broadcasted_iota(jnp.int32, value.shape, 2)
    if up:
        rolled = pltpu.roll(value, LANES - 1, 2)
        return jnp.where(lane == LANES - 1, jnp.concatenate([rolled[1:], rolled[:1]], axis=0), rolled)
    rolled = pltpu.roll(value, 1, 2)
    return jnp.where(lane == 0, jnp.concatenate([rolled[-1:], rolled[:-1]], axis=0), rolled)


def lane_gather(value, index):
    return jnp.take_along_axis(value, index, axis=1)


def next_chunk():
    lane = lane_iota()
    return jnp.where(lane < 64, lane + 64, jnp.where(lane == 127, 0, lane - 63))


def previous_chunk():
    lane = lane_iota()
    return jnp.where(lane >= 64, lane - 64, jnp.where(lane == 0, 127, lane + 63))


def swap_tiles_and_lanes(tiles):
    lane = lane_iota()
    for bit in range(4):
        width = 4 << bit
        high = (lane // width) % 2 == 1
        out = list(tiles)
        for m in range(16):
            if not m >> bit & 1:
                a, b = tiles[m], tiles[m | 1 << bit]
                out[m] = jnp.where(high, pltpu.roll(b, width, 1), a)
                out[m | 1 << bit] = jnp.where(high, b, pltpu.roll(a, LANES - width, 1))
        tiles = out
    return tiles


def to_chunks(tiles):
    lane = lane_iota()
    index = ((lane % 4) * 2 + lane // 64) * 16 + (lane % 64) // 4
    return swap_tiles_and_lanes([lane_gather(t, index) for t in tiles])


def from_chunks(tiles):
    lane = lane_iota()
    block = lane // 16
    index = (block % 2) * 64 + (lane % 16) * 4 + block // 2
    return [lane_gather(t, index) for t in swap_tiles_and_lanes(tiles)]


def coarse_step(count, w_in, w_out, win, values, extra, taps, sums, parts):
    lanes = win.shape[0]
    off = REACH - 4 * count
    at = [pl.ds(off + q, 8, stride=count) for q in range(count)]

    def tiles(q):
        return slice(lanes * q, lanes * q + lanes)

    for q in range(count):
        x = win[:, at[q], :]
        for dx, v in enumerate((lane_shifted(x, False), x, lane_shifted(x, True))):
            for dy in range(3):
                place = q + 1 - dy
                if place < 0:
                    taps[dy * 3 + dx, tiles(count - 1)] = pltpu.roll(v, 7, 1)
                elif place >= count:
                    taps[dy * 3 + dx, tiles(0)] = pltpu.roll(v, 1, 1)
                else:
                    taps[dy * 3 + dx, tiles(place)] = v
    total = lanes * count
    group = GROUP

    def few(i, _):
        some = pl.ds(jnp.minimum(i * group, total - group), group)
        x = taps[:, some]
        acc = None
        for h in range(8):
            hidden = jnp.tanh(jnp.sum(w_in[h][:, None] * x, axis=0))
            term = w_out[h][:, None] * hidden[None]
            acc = term if acc is None else acc + term
        sums[:, some] = acc
        return 0

    lax.fori_loop(0, -(-total // group), few, 0)
    for q in range(count):
        for dy in range(3):
            low = lane_shifted(sums[dy * 3, tiles(q)], False)
            high = lane_shifted(sums[dy * 3 + 2, tiles(q)], True)
            v = low + high + sums[dy * 3 + 1, tiles(q)]
            parts[dy, q + 1] = v
            if q == 0 and dy == 2:
                parts[dy, count + 1] = pltpu.roll(v, 7, 1)
            if q == count - 1 and dy == 0:
                parts[dy, 0] = pltpu.roll(v, 1, 1)
    for q in range(count):
        g = win[:, at[q], :] + (parts[0, q] + parts[1, q + 1] + parts[2, q + 2])
        values[:, at[q], :] = g
        if extra is not None:
            win[:, at[q], :] = g + extra(off + q, count)


def own_columns(value):
    rolled = pltpu.roll(value, 64, 2)
    lane = lax.broadcasted_iota(jnp.int32, (2, 8, LANES), 2)
    return jnp.where(lane < 64, rolled[:2], rolled[1:])


def fine_stage(src, dst, base, pcoef, qcoef, force, off, count, scale, of_base):
    at = [pl.ds(off + q, 8, stride=count) for q in range(-1, count + 1)]

    def block(first, size):
        centre = pl.ds(first, size)
        wide = [src[pl.ds(first - 1, size + 2), a, :] for a in at[1:-1]]
        column = [src[centre, at[0], :]] + [x[1:-1] for x in wide] + [src[centre, at[-1], :]]
        results = []
        for q in range(count):
            slot = (centre, at[q + 1], slice(None))
            left, right = wide[q][:-2], wide[q][2:]
            above, below = column[q + 2], column[q]
            t = pcoef[slot] * (right - left) + qcoef[slot] * (above - below) + (left + below)
            if scale != 1.0:
                t = scale * t
            here = column[q + 1] if src is base else base[slot]
            t = t + (of_base * here + force[slot])
            dst[slot] = t
            results.append(t)
        return results

    last = block(CHUNK - 1, 2)
    first = block(1, 2)
    ahead, back = next_chunk(), previous_chunk()
    for q in range(count):
        dst[0, at[q + 1], :] = lane_gather(last[q][1], back)
        dst[CHUNK + 1, at[q + 1], :] = lane_gather(first[q][0], ahead)
    group = 6 if count > 6 else 10

    def body(g, _):
        block(3 + g * group, group)
        return 0

    lax.fori_loop(0, (CHUNK - 4) // group, body, 0)


def fine_run(state, one, two, pcoef, qcoef, force):
    of_w, _ = fine_weights()
    for step in range(STEPS):
        count = 9 if step == 0 else 8 - step
        off = 4 if step == 0 else PAD + 4 * step
        shared = (state, pcoef, qcoef)
        fine_stage(state, one, *shared, force.at[3], off, count, 1.0, of_w[3] / of_w[4])
        fine_stage(one, two, *shared, force.at[2], off, count, 1.0, of_w[2] / of_w[4])
        fine_stage(two, one, *shared, force.at[1], off, count, 1.0, of_w[1] / of_w[4])
        fine_stage(one, state, *shared, force.at[0], off, count, of_w[4], of_w[0])


def ghosts(ref):
    ahead, back = next_chunk(), previous_chunk()
    for r in range(PAD, TALL - PAD, 8):
        ref[0, r : r + 8, :] = lane_gather(ref[CHUNK, r : r + 8, :], back)
        ref[CHUNK + 1, r : r + 8, :] = lane_gather(ref[1, r : r + 8, :], ahead)


def coefficients(stream, forcing, pcoef, qcoef, force):
    of_w, of_f = fine_weights()
    ghosts(stream)
    count = 9
    at = [pl.ds(4 + q, 8, stride=count) for q in range(-1, count + 1)]

    group = 4

    def body(g, _):
        first = 1 + g * group
        c = pl.ds(first, group)
        wide = [stream[pl.ds(first - 1, group + 2), a, :] for a in at[1:-1]]
        x = [stream[c, at[0], :]] + [v[1:-1] for v in wide] + [stream[c, at[-1], :]]
        for q in range(count):
            a = at[q + 1]
            pcoef[c, a, :] = 0.5 - 1.25 * (x[q + 2] - x[q])
            qcoef[c, a, :] = 0.5 + 1.25 * (wide[q][2:] - wide[q][:-2])
            f = forcing[c, a, :]
            force[0, c, a, :] = of_f[0] * f
            for k in range(1, 4):
                force[k, c, a, :] = (of_f[k] / of_w[4]) * f
        return 0

    lax.fori_loop(0, CHUNK // group, body, 0)


def natural_to_rows(source, nat):
    for c in range(64):
        nat[c * PITCH : c * PITCH + INNER, :] = source[:, c * LANES : (c + 1) * LANES]


def rows_to_chunks(nat, lam):
    low = lax.broadcasted_iota(jnp.int32, (64, LANES), 1) < 64
    for i in range(INNER // 2):
        j = i + INNER // 2
        at_i, at_j = pl.ds(i, 64, stride=PITCH), pl.ds(j, 64, stride=PITCH)
        flipped = jnp.concatenate([nat[at_i, :], nat[at_j, :]], axis=0).T
        top, bottom = flipped[:64], flipped[64:]
        lam[at_i, :] = jnp.where(low, top, pltpu.roll(bottom, 64, 1))
        lam[at_j, :] = jnp.where(low, pltpu.roll(top, 64, 1), bottom)


def chunks_to_rows(lam, nat):
    low = lax.broadcasted_iota(jnp.int32, (64, LANES), 1) < 64
    for i in range(INNER // 2):
        j = i + INNER // 2
        at_i, at_j = pl.ds(i, 64, stride=PITCH), pl.ds(j, 64, stride=PITCH)
        x, y = lam[at_i, :], lam[at_j, :]
        top = jnp.where(low, x, pltpu.roll(y, 64, 1))
        bottom = jnp.where(low, pltpu.roll(x, 64, 1), y)
        flipped = jnp.concatenate([top, bottom], axis=0).T
        nat[at_i, :] = flipped[:64]
        nat[at_j, :] = flipped[64:]


def store_own(lam, ref):
    for c in range(CHUNK):
        ref[1 + c, OWN : OWN + INNER, :] = lam[c * PITCH : c * PITCH + INNER, :]


def load_own(ref, lam):
    for c in range(CHUNK):
        lam[c * PITCH : c * PITCH + INNER, :] = ref[1 + c, OWN : OWN + INNER, :]


def spaced_tiles(tiles, rolled):
    lane = lane_iota()
    turned = [pltpu.roll(t, 64, 1) for t in tiles]
    for k in range(BLOCKS):
        v = jnp.where(lane < 64, turned[k - 1], turned[k])
        rolled[k] = v
        if k < 2:
            rolled[BLOCKS + k] = v


def block_means(state):
    tiles = []
    for m in range(BLOCKS):
        four = [state[1 + 4 * m : 5 + 4 * m, pl.ds(OWN + q, 8, stride=4), :] for q in range(4)]
        tiles.append(0.0625 * jnp.sum((four[0] + four[1]) + (four[2] + four[3]), axis=0))
    return from_chunks(tiles)


def coarse_in_chunks(pieces, coarse):
    for half in range(2):
        at = pl.ds(half, 8, stride=2)
        tiles = to_chunks([pieces[m // 2, m % 2, at, :] for m in range(BLOCKS)])
        for m in range(BLOCKS):
            coarse[m, at, :] = tiles[m]


def spread_coarse(coarse, base, state):
    upper = lax.broadcasted_iota(jnp.int32, (8, LANES), 0) < 4

    def body(m, _):
        c = pl.ds(4 * m, 4)
        for r in range(8):
            v = jnp.where(upper, coarse[m, 2 * r : 2 * r + 1, :], coarse[m, 2 * r + 1 : 2 * r + 2, :])[None]
            old = base(c, r)
            v = jnp.broadcast_to(v, (4, 8, LANES)) if old is None else old + v
            state[pl.ds(4 * m + 1, 4), PAD + 8 * r : PAD + 8 * r + 8, :] = v
        return 0

    lax.fori_loop(0, BLOCKS, body, 0)


SLOTS = 64
GROUP = 2


def kernel(
    conv_in, conv_out, vort_hbm, stream_hbm, force_hbm, out,
    inputs, nat, lam, fields, state, one, two, pcoef, qcoef, force,
    start, win, old, new, taps, sums, parts, w_in, w_out,
    rolled, means, sent, got, edge, coarse, packed,
    in_sem, send_sem, recv_sem,
):
    t, z = lax.axis_index("tm"), lax.axis_index("space")
    slabs = lax.axis_size("space")
    parity = lax.rem(t, 2)
    used = [0]

    def slot_of(k):
        return lax.rem(t + k, SLICES)

    def slab_of(d):
        return lax.rem(z + d + slabs, slabs)

    def remote(src, dst, to):
        n = used[0]
        used[0] += 1
        return pltpu.make_async_remote_copy(
            src_ref=src, dst_ref=dst, send_sem=send_sem.at[n], recv_sem=recv_sem.at[n],
            device_id=to, device_id_type=MESH,
        )

    def start_all(copies):
        for c in copies:
            c.start()

    def recv_all(copies):
        for c in copies:
            c.wait_recv()

    def sent_all(copies):
        for c in copies:
            c.wait_send()

    loads = [
        pltpu.make_async_copy(ref, inputs.at[i], in_sem.at[i])
        for i, ref in enumerate((vort_hbm, stream_hbm, force_hbm))
    ]
    start_all(loads)
    barrier = pltpu.get_barrier_semaphore()
    peers = [(slot_of(k), z) for k in range(1, SLICES)] + [(t, slab_of(d)) for d in (-3, -2, -1, 1, 2, 3)]
    for p in peers:
        pl.semaphore_signal(barrier, inc=1, device_id=p, device_id_type=MESH)
    for h in range(8):
        for k in range(9):
            w_in[h, k] = jnp.full((8, LANES), conv_in[h, k // 3, k % 3], F32)
            w_out[h, k] = jnp.full((8, LANES), 0.5 * conv_out[h, k // 3, k % 3], F32)

    loads[0].wait()
    natural_to_rows(inputs.at[0], nat)
    for c in range(64):
        four = [nat[pl.ds(c * PITCH + q, 8, stride=4), :] for q in range(4)]
        m, k = c // 4, c % 4
        packed[m * 8 : m * 8 + 8, k * LANES : (k + 1) * LANES] = (four[0] + four[1]) + (four[2] + four[3])
    averages = jnp.where(
        lax.broadcasted_iota(jnp.int32, (4 * LANES, LANES), 0) // 4
        == lax.broadcasted_iota(jnp.int32, (4 * LANES, LANES), 1), 0.0625, 0.0,
    ).astype(F32)
    first = jnp.dot(packed[...], averages, precision=HIGH, preferred_element_type=F32)
    spaced_tiles([first[m * 8 : m * 8 + 8] for m in range(BLOCKS)], rolled.at[0])
    mine = pl.ds(2 * t, 3)
    pl.semaphore_wait(barrier, len(peers))
    near = [
        remote(rolled.at[0, mine], start.at[:, REACH - 4 - 8 * d : REACH + 4 - 8 * d, :], (t, slab_of(d)))
        for d in (-1, 1, -2, 2, -3, 3)
    ]
    start_all(near)
    start[:, REACH - 4 : REACH + 4, :] = rolled[0, mine]

    @pl.when(t <= 1)
    def _():
        rows_to_chunks(nat, lam)
        store_own(lam, state)

    for i in (1, 2):
        loads[i].wait()
        natural_to_rows(inputs.at[i], nat)
        rows_to_chunks(nat, lam)
        store_own(lam, fields.at[i - 1])
    inside = slice(1, CHUNK + 1)
    low, high = slice(OWN - HALO, OWN), slice(OWN + INNER, OWN + INNER + HALO)
    first_rows, last_rows = slice(OWN, OWN + HALO), slice(OWN + INNER - HALO, OWN + INNER)
    across = [
        remote(fields.at[parity, inside, last_rows], fields.at[parity, inside, low], (t, slab_of(1))),
        remote(fields.at[parity, inside, first_rows], fields.at[parity, inside, high], (t, slab_of(-1))),
    ]
    sibling = (t + 1 - 2 * parity, z)
    shared = [
        remote(fields.at[parity, inside, rows], fields.at[parity, inside, rows], sibling) for rows in (low, high)
    ]
    early = [
        remote(state.at[inside, last_rows], state.at[inside, low], (t, slab_of(1))),
        remote(state.at[inside, first_rows], state.at[inside, high], (t, slab_of(-1))),
    ]

    @pl.when(t <= 1)
    def _():
        start_all(early)

    start_all(across)

    recv_all(near)
    win[...] = start[...]
    scratch = (taps, sums, parts)

    def keep(phase, n, read, rows):
        for r in range(0, rows, 8):
            sent[phase, n, :, r : r + 8, :] = own_columns(read(REACH - rows // 2 + r))

    def rows_of(ref):
        return lambda r: ref[:, r : r + 8, :]

    def nothing(phase, n):
        sent[phase, n] = jnp.zeros(sent.shape[2:], F32)

    def out_copies(phase, shift, rows):
        return [
            remote(
                sent.at[phase, lax.rem(slot_of(k) + shift, SLICES), :, 0:rows],
                got.at[phase, t, :, 0:rows],
                (slot_of(k), z),
            )
            for k in range(1, SLICES)
        ]

    def keep_own(phase, shift):
        got[phase, t] = sent[phase, lax.rem(t + shift, SLICES)]

    plain = lambda row, count: 0.0
    nothing(0, 0)
    nothing(0, 7)
    for n in range(6):
        coarse_step(-(-(44 - 4 * n) // 8), w_in, w_out, win, old.at[n], plain, *scratch)
        keep(0, n + 1, rows_of(win), 16)
    deliver = out_copies(0, SLICES - 1, 16)
    start_all(deliver)
    keep_own(0, SLICES - 1)
    for n in (6, 7):
        coarse_step(-(-(44 - 4 * n) // 8), w_in, w_out, win, old.at[n], plain if n < 7 else None, *scratch)

    recv_all(across)
    start_all(shared)
    recv_all(shared)
    coefficients(fields.at[0], fields.at[1], pcoef, qcoef, force)
    recv_all(deliver)

    @pl.when(t <= 1)
    def _():
        recv_all(early)
        sent_all(early)

    @pl.when(t > 1)
    def _():
        coarse_in_chunks(got.at[0], coarse)
        spread_coarse(coarse, lambda c, r: None, state)

    ghosts(state)
    fine_run(state, one, two, pcoef, qcoef, force)

    def share_means(phase, shift, plus_one, plus_two):
        spaced_tiles(block_means(state), rolled.at[phase + 1])
        place = lax.rem(t + shift, SLICES)
        middle = slice(16, 24)
        copies = [
            remote(rolled.at[phase + 1, pl.ds(2 * slot_of(k), 3)], means.at[phase, place, :, middle], (slot_of(k), z))
            for k in range(1, SLICES)
        ]
        start_all(copies)
        means[phase, place, :, middle, :] = rolled[phase + 1, pl.ds(2 * t, 3)]
        around = [
            remote(
                means.at[phase, slice(*slots), :, middle],
                means.at[phase, slice(*slots), :, 16 - 8 * d : 24 - 8 * d],
                (t, slab_of(d)),
            )
            for d, slots in ((-1, plus_one), (1, plus_one), (-2, plus_two), (2, plus_two))
        ]
        return copies, around

    to_slots, around = share_means(0, SLICES - 1, (0, 7), (0, 4))
    bulk = [
        [
            remote(state.at[part, last_rows], edge.at[0, keep_part], (t, slab_of(1))),
            remote(state.at[part, first_rows], edge.at[1, keep_part], (t, slab_of(-1))),
        ]
        for part, keep_part in (
            (slice(1, 1 + CHUNK // 2), slice(0, CHUNK // 2)),
            (slice(1 + CHUNK // 2, 1 + CHUNK), slice(CHUNK // 2, CHUNK)),
        )
    ]
    start_all(bulk[0])
    recv_all(to_slots)
    start_all(around)
    start_all(bulk[1])
    recv_all(around)

    nothing(1, 0)
    nothing(1, 7)
    win[:, 8:48, :] = means[0, 0]

    def corrected(phase, n, before):
        def extra(row, count):
            there = pl.ds(row - 8, 8, stride=count)
            return means[phase, n, :, there, :] - before[n, :, pl.ds(row, 8, stride=count), :]

        return extra

    def change(a, b):
        return lambda r: a[:, r : r + 8, :] - b[:, r : r + 8, :]

    for n in range(1, 7):
        coarse_step(-(-(44 - 4 * n) // 8), w_in, w_out, win, new.at[n], corrected(0, n, old), *scratch)
        keep(1, n, change(new.at[n], old.at[n]), 16)
    deliver_2 = out_copies(1, SLICES - 1, 16)
    start_all(deliver_2)
    keep_own(1, SLICES - 1)
    coarse_step(-(-(44 - 4 * 7) // 8), w_in, w_out, win, new.at[7], None, *scratch)

    for part in bulk:
        recv_all(part)
        sent_all(part)
    recv_all(deliver_2)

    @pl.when(t > 0)
    def _():
        coarse_in_chunks(got.at[1], coarse)

        def base(c, r):
            if r < 2:
                return edge[0, c, 8 * r : 8 * r + 8, :]
            if r >= 6:
                return edge[1, c, 8 * (r - 6) : 8 * (r - 6) + 8, :]
            return state[pl.ds(c.start + 1, 4), PAD + 8 * r : PAD + 8 * r + 8, :]

        spread_coarse(coarse, base, state)
        ghosts(state)
        fine_run(state, one, two, pcoef, qcoef, force)

    to_slots_2, around_2 = share_means(1, 0, (1, 7), (1, 3))
    load_own(state, lam)
    chunks_to_rows(lam, nat)
    recv_all(to_slots_2)
    start_all(around_2)
    recv_all(around_2)

    nothing(2, 0)
    nothing(2, 1)
    win[:, 8:48, :] = means[1, 1]
    for n in range(2, 8):
        coarse_step(
            -(-(40 - 4 * n) // 8), w_in, w_out, win, old.at[n], corrected(1, n, new) if n < 7 else None, *scratch
        )
        keep(2, n, change(old.at[n], new.at[n]), 8)
    deliver_3 = out_copies(2, 0, 8)
    start_all(deliver_3)
    keep_own(2, 0)
    recv_all(deliver_3)

    copies = jnp.where(
        lax.broadcasted_iota(jnp.int32, (LANES, 4 * LANES), 0)
        == lax.broadcasted_iota(jnp.int32, (LANES, 4 * LANES), 1) // 4, 1.0, 0.0,
    ).astype(F32)
    delta = jnp.concatenate([got[2, m // 2, m % 2, 0:8, :] for m in range(BLOCKS)], axis=0)
    packed[...] = jnp.dot(delta, copies, precision=HIGH, preferred_element_type=F32)
    for c in range(64):
        m, k = c // 4, c % 4
        v = packed[m * 8 : m * 8 + 8, k * LANES : (k + 1) * LANES]
        for q in range(4):
            at = pl.ds(c * PITCH + q, 8, stride=4)
            nat[at, :] = nat[at, :] + v
        out[:, c * LANES : (c + 1) * LANES] = nat[c * PITCH : c * PITCH + INNER, :]
    for group in (near, across, shared, deliver, to_slots, around, deliver_2, to_slots_2, around_2, deliver_3):
        sent_all(group)


def body(vorticity, stream, forcing, conv_in, conv_out):
    rows, cols = vorticity.shape
    whole = (CHUNK + 2, TALL, LANES)
    smem = pl.BlockSpec(memory_space=pltpu.SMEM)
    anywhere = pl.BlockSpec(memory_space=pl.ANY)
    window = (3, WINDOW, LANES)
    shapes = [
        (3, rows, cols), (64 * PITCH, LANES), (CHUNK * PITCH, LANES), (2,) + whole, whole, whole, whole, whole, whole,
        (4,) + whole, window, window, (SLICES,) + window, (SLICES,) + window,
        (9, 18, 8, LANES), (9, 18, 8, LANES), (3, 8, 3, 8, LANES), (8, 9, 8, LANES), (8, 9, 8, LANES),
        (3, BLOCKS + 2, 8, LANES), (2, SLICES, 3, 40, LANES), (3, SLICES, 2, 16, LANES), (3, SLICES, 2, 16, LANES),
        (2, CHUNK, HALO, LANES), (BLOCKS, 16, LANES), (8 * BLOCKS, 4 * LANES),
    ]
    out = pl.pallas_call(
        kernel,
        name="parareal",
        out_shape=jax.ShapeDtypeStruct((rows, cols), F32),
        in_specs=[smem, smem, anywhere, anywhere, anywhere],
        out_specs=pl.BlockSpec(memory_space=VMEM),
        scratch_shapes=[VMEM(s, F32) for s in shapes]
        + [pltpu.SemaphoreType.DMA((3,)), pltpu.SemaphoreType.DMA((SLOTS,)), pltpu.SemaphoreType.DMA((SLOTS,))],
        compiler_params=pltpu.CompilerParams(vmem_limit_bytes=62 * 2**20, collective_id=0, has_side_effects=True),
    )(conv_in, conv_out, vorticity, stream, forcing)
    return out[None]


def solution(mesh):
    placed = (P("space", None), P("space", None), P("space", None), P(), P())
    return jax.shard_map(
        body, mesh=mesh, in_specs=placed, out_specs=P("tm", "space", None), check_vma=False
    )
```

time: 985 us -> 113 us (0.11); the launches traced: 974 us -> 112 us
  starting transfers between devices: 366 us -> 0 us
  waiting for transfers between devices: 219 us -> 0 us
  local copies, waits for them, and re-layouts: 223 us -> 4.35 us
  other arithmetic: 161 us -> 0 us
  Pallas kernels: 0 us -> 108 us
    ppermute x136 -> x0, starting transfers between devices: 366 us -> none  [the longest x57 166 us: with_halo(): after = lax.ppermute(first, axis, down)]
    ppermute x136 -> x0, waiting for transfers between devices: 219 us -> none  [the longest x57 142 us: with_halo(): before = lax.ppermute(last, axis, up)]
    reshape x12 -> x0, local copies, waits for them, and re-layouts: 170 us -> none  [the longest x3 156 us: restrict(): blocks = values.reshape((row_count // 4, 4, col_count // 4, 4))]
    pallas_call x0 -> x1, Pallas kernels: none -> 108 us  [body(): pl.pallas_call(kernel, name='parareal', out_shape=jax.ShapeDtypeStruct((r...]
    reduce_sum x171 -> x0, other arithmetic: 70.4 us -> none  [the longest x3 36.6 us: restrict(): return jnp.mean(blocks, axis=(-3, -1))]
    add x54 -> x0, other arithmetic: 51.6 us -> none  [the longest x8 24.2 us: body(): fine_state + time_step / 6.0 * (slope_one + 2.0 * slope_two + 2.0 * slope...]
    slice x267 -> x0, local copies, waits for them, and re-layouts: 40.3 us -> none  [the longest x48 15.4 us: collect(): jnp.roll(hidden[:, row_shift:row_shift + row_count], 1 - col_shift, axis=-1)]
    tanh x24 -> x0, other arithmetic: 18.7 us -> none  [coarse_advance(): hidden = jnp.tanh(spread(padded, conv_in))]
  transfers between devices with their start and end apart: 136 -> 0, of which waited for: 110 -> 0; matrix products, arithmetic and copies ran while one was open for 2% -> 0% of each run, Pallas kernels for 0% -> 0%
where the time goes in v1:
time: 113 us; the launch traced here: 112 us
  Pallas kernels  108 us (96%)
  local copies, waits for them, and re-layouts  4.35 us (4%)
    pallas_call x1, Pallas kernels, body(): pl.pallas_call(kernel, name='parareal', out_shape=jax.ShapeDtypeStruct((r...  108 us
    unnamed x5, local copies, waits for them, and re-layouts  4.35 us

profile of v1, /device:TPU:1, one launch (start us, length us, event | category | flops | bytes accessed | tf_op | source)
XLA Modules:
  0.0 112.3 jit_solution(5533428723634197716)
XLA Ops:
  0.0 0.0 copy-start
  0.0 1.4 %copy.6.conv_in = f32[8,3,3]{2,1,0:T(4,128)} copy(f32[8,3,3]{0,2,1:T(4,128)} %param.8) | data formatting | bytes 576 | tf_op args[3]
  1.4 0.0 copy-done
  1.4 0.7 copy.7.conv_out
  2.1 107.9 %parareal.1 = f32[32,8192]{1,0:T(8,128)} custom-call(f32[8,3,3]{2,1,0:T(4,128)} %copy.6.conv_in, f32[8,3,3]{2,1,0:T(4,128)} %copy.7.conv_out, f32[32,8192]{1,0:T(8,128)} %vort_hbm.1, f32[32,8192]{1,0:T(8,128)} %stream_hbm.1, f32[32,8192]{1,0:T(8,128)} %force_hbm.1), custom_call_target="tpu_custom_call" | custom-call | tf_op jit(solution)/shard_map/parareal/pallas_call | solution.py:608
  110.0 2.3 %copy.9 = f32[1,32,8192]{2,1,0:T(8,128)} copy(f32[1,32,8192]{2,1,0:T(8,128)} %bitcast.1) | data formatting | bytes 2097152
Async XLA Ops:
  0.0 1.4 %copy-start = (f32[8,3,3]{0,2,1:T(4,128)S(1)}, f32[8,3,3]{0,2,1:T(4,128)}, u32[]{:S(2)}) copy-start(f32[8,3,3]{0,2,1:T(4,128)} %param.9) | copy-start | bytes 868
